TPU v7x, 32 devices: a whole 2x2x4 slice. The times are simulated.
32 devices in a mesh: pipe: 4 (over z), dp: 4 (over x, core), fsdp: 2 (over y).
Axes of the slice: x: 2, y: 2, z: 4, core: 2. Of those that a mesh axis runs over, the one named last changes fastest.
Arguments:
- layer_inputs: bfloat16 [4, 2, 2048, 4096], P('pipe', None, ('dp', 'fsdp')), may hold values from -6 to 6
- key_grads: bfloat16 [4, 2, 2048, 512], P('pipe', None, ('dp', 'fsdp')), may hold values from -12 to 12
- token_counts: int32 [4, 16], P('pipe', ('dp', 'fsdp')), may hold values from 1 to 256, 2048 in all within a row
- master_weight: float32 [4, 4096, 512], P('pipe', 'fsdp'), may hold values from -0.09375 to 0.09375
- first_moment: float32 [4, 4096, 512], P('pipe', 'fsdp'), may hold values from -3 to 3
- second_moment: float32 [4, 4096, 512], P('pipe', 'fsdp'), may hold values from 0.05 to 2
Outputs:
- input_grads: bfloat16 [4, 2, 2048, 4096], P('pipe', None, ('dp', 'fsdp'))
- new_weight: float32 [4, 4096, 512], P('pipe', 'fsdp')
- new_first: float32 [4, 4096, 512], P('pipe', 'fsdp')
- new_second: float32 [4, 4096, 512], P('pipe', 'fsdp')
Inputs may be any that keep to these rules, and one draw needn't show every extreme that they name: `token_counts`: in each section the counts sum to 2048, and some microbatch of each section is full.
All inputs are finite; a program needn't handle non-finite values. No bound on the sum of `token_counts` on one device may be relied on, other than what follows from the above.
Results may differ from a plain program's by a relative error of at most 0.00105.
The roundings to bfloat16 on the way count: a program that leaves them out, or rounds other values in their place, can miss the bound.
Values may be sent and summed in bfloat16 or wider, within the bound.
A program may use at most 128 MiB of HBM per device.

v0:
```python
import jax
import jax.numpy as jnp
from jax import lax
from jax.sharding import PartitionSpec as P

beta_one = 0.9
beta_two = 0.95
learn_rate = 0.01
decay_rate = 0.1
adam_eps = 1e-08
loss_scale = 256.0
first_bias = 1.0 - 0.9**10
second_bias = 1.0 - 0.95**10


def passed_along(array, axis, by):
    count = lax.axis_size(axis)
    pairs = [(i, i + by) for i in range(count) if 0 <= i + by < count]
    return lax.ppermute(array, axis, pairs)


def adamw_update(weight_part, first_part, second_part, gradient):
    first_next = beta_one * first_part + (1.0 - beta_one) * gradient
    second_next = beta_two * second_part + (1.0 - beta_two) * gradient * gradient
    first_hat = first_next / first_bias
    second_hat = second_next / second_bias
    weight_next = weight_part - learn_rate * (
        first_hat / (jnp.sqrt(second_hat) + adam_eps) + decay_rate * weight_part
    )
    return (weight_next, first_next, second_next)


def local(layer_inputs, key_grads, token_counts, master_weight, first_moment, second_moment):
    stored = layer_inputs[0]
    cotangent = key_grads[0]
    counts_here = token_counts[0]
    micro_count, token_count, feature_count = stored.shape
    key_width = cotangent.shape[-1]
    positions = jnp.arange(token_count, dtype=jnp.int32)
    live_rows = positions[None, :] < counts_here[:, None]
    masked = jnp.where(live_rows[:, :, None], cotangent, jnp.zeros_like(cotangent))
    weight_half = master_weight.astype(jnp.bfloat16)
    terms = jnp.einsum(
        "mtk,rk->mtr",
        masked,
        lax.all_gather(weight_half, "fsdp", axis=1, tiled=True)[0],
        preferred_element_type=jnp.float32,
    )
    section_total = lax.axis_size("pipe")
    section_index = lax.axis_index("pipe")
    turn_total = section_total - 1 + micro_count
    incoming = jnp.zeros((token_count, feature_count), jnp.bfloat16)
    grad_buffer = jnp.zeros((micro_count, token_count, feature_count), jnp.bfloat16)
    for turn_index in range(turn_total):
        micro_slot = turn_index - (section_total - 1 - section_index)
        active = jnp.logical_and(micro_slot >= 0, micro_slot < micro_count)
        picked = jnp.clip(micro_slot, 0, micro_count - 1)
        section_term = lax.dynamic_index_in_dim(terms, picked, 0, keepdims=False)
        result = (incoming.astype(jnp.float32) + section_term).astype(jnp.bfloat16)
        current = lax.dynamic_index_in_dim(grad_buffer, picked, 0, keepdims=False)
        grad_buffer = lax.dynamic_update_index_in_dim(
            grad_buffer, jnp.where(active, result, current), picked, 0
        )
        if turn_index + 1 < turn_total:
            incoming = passed_along(result, "pipe", -1)
    block_rows = 128
    shard_rows = master_weight.shape[1]
    first_row = jnp.int32(0)
    running = jnp.zeros((lax.axis_size("fsdp") * shard_rows, key_width), jnp.float32)
    for micro_index in range(micro_count):
        passes = (counts_here[micro_index] + block_rows - 1) // block_rows

        def accumulate(block_index, partial_sum, micro_index=micro_index):
            offset = (block_index * block_rows).astype(jnp.int32)
            inputs_block = lax.dynamic_slice(
                stored[micro_index],
                (offset, jnp.asarray(first_row, jnp.int32)),
                (block_rows, lax.axis_size("fsdp") * shard_rows),
            )
            grads_block = lax.dynamic_slice_in_dim(masked[micro_index], offset, block_rows, 0)
            return partial_sum + lax.dot_general(
                inputs_block,
                grads_block,
                (((0,), (0,)), ((), ())),
                preferred_element_type=jnp.float32,
            )

        running = lax.fori_loop(0, passes, accumulate, running)
    partial_value = lax.psum_scatter(
        running.astype(jnp.bfloat16), "fsdp", scatter_dimension=0, tiled=True
    )
    gradient = lax.psum(partial_value, "dp").astype(jnp.float32) / loss_scale
    new_weight, new_first, new_second = adamw_update(
        master_weight[0], first_moment[0], second_moment[0], gradient
    )
    return (grad_buffer[None], new_weight[None], new_first[None], new_second[None])


def solution(mesh):
    in_specs = (
        P("pipe", None, ("dp", "fsdp"), None),
        P("pipe", None, ("dp", "fsdp"), None),
        P("pipe", ("dp", "fsdp")),
        P("pipe", "fsdp", None),
        P("pipe", "fsdp", None),
        P("pipe", "fsdp", None),
    )
    out_specs = (
        P("pipe", None, ("dp", "fsdp"), None),
        P("pipe", "fsdp", None),
        P("pipe", "fsdp", None),
        P("pipe", "fsdp", None),
    )
    return jax.shard_map(local, mesh=mesh, in_specs=in_specs, out_specs=out_specs, check_vma=False)
```

profile of v0, /device:TPU:0, one launch (start us, length us, event | category | flops | bytes accessed | tf_op | source)
XLA Modules:
  0.0 301.9 jit_solution(5821186887589029161)
XLA Ops:
  7.2 3.8 %convert_element_type.42 = bf16[1,2048,512]{2,1,0:T(8,128)(2,1)} convert(f32[1,2048,512]{2,1,0:T(8,128)} %param.13) | non-fusion elementwise | flops 1048576 | bytes 6291456 | tf_op jit(solution)/shard_map/convert_element_type | solution.py:42
  13.3 4.3 %broadcast_in_dim.58 = f32[4096,512]{1,0:T(8,128)} broadcast(f32[]{:T(128)} %constant.122.clone.1), dimensions={} | broadcast | bytes 8388612 | tf_op jit(solution)/shard_map/broadcast_in_dim | solution.py:69
  17.6 10.8 %while.20 = (s32[]{:T(128)}, f32[4096,512]{1,0:T(8,128)}, s32[]{:T(128)}, bf16[2,256,4096]{2,1,0:T(8,128)(2,1)}, bf16[2,256,512]{2,1,0:T(8,128)(2,1)S(1)}, /*index=5*/s32[]{:T(128)}, s32[]{:T(128)}, s32[]{:T(128)}, s32[]{:T(128)}) while((s32[]{:T(128)}, f32[4096,512]{1,0:T(8,128)}, s32[]{:T(128)}, bf16[2,256,4096]{2,1,0:T(8,128)(2,1)}, ...), condition=%wide.region_1.2_spmd, body=%wide.region_0.1_spmd.sunk | while | flops 538968064 | bytes 22676620 | solution.py:88
  17.6 1.7 slice.28
  19.3 9.0 %convolution_add_fusion.4 = f32[4096,512]{1,0:T(8,128)} fusion(f32[4096,512]{1,0:T(8,128)} %get-tuple-element.169, bf16[1,256,4096]{2,1,0:T(8,128)(2,1)S(1)} %slice.28, s32[]{:T(128)S(6)} %select_n.118, bf16[1,256,512]{2,1,0:T(8,128)(2,1)S(1)} %slice.29), kind=kOutput, calls=%fused_computation.clone.1 | convolution fusion | flops 538968064 | bytes 17957888 | tf_op jit(solution)/shard_map/while/body/dot_general | solution.py:81
  28.4 9.7 %while.21 = (s32[]{:T(128)}, f32[4096,512]{1,0:T(8,128)}, s32[]{:T(128)}, bf16[2,256,4096]{2,1,0:T(8,128)(2,1)}, bf16[2,256,512]{2,1,0:T(8,128)(2,1)S(1)}, /*index=5*/s32[]{:T(128)}, s32[]{:T(128)}, s32[]{:T(128)}, s32[]{:T(128)}) while((s32[]{:T(128)}, f32[4096,512]{1,0:T(8,128)}, s32[]{:T(128)}, bf16[2,256,4096]{2,1,0:T(8,128)(2,1)}, ...), condition=%wide.region_3.4_spmd, body=%wide.region_2.3_spmd.sunk | while | flops 538968064 | bytes 22676620 | solution.py:88
  28.4 1.7 slice.30
  30.1 7.9 %convolution_add_fusion.5 = f32[4096,512]{1,0:T(8,128)} fusion(f32[4096,512]{1,0:T(8,128)} %get-tuple-element.196, bf16[1,256,4096]{2,1,0:T(8,128)(2,1)S(1)} %slice.30, s32[]{:T(128)S(6)} %select_n.119, bf16[1,256,512]{2,1,0:T(8,128)(2,1)S(1)} %slice.31), kind=kOutput, calls=%fused_computation.6.clone.1 | convolution fusion | flops 538968064 | bytes 17957888 | tf_op jit(solution)/shard_map/while/body/dot_general | solution.py:81
  38.0 5.9 %convert_element_type.53 = bf16[4096,512]{1,0:T(8,128)(2,1)} convert(f32[4096,512]{1,0:T(8,128)} %get-tuple-element.61) | non-fusion elementwise | flops 2097152 | bytes 12582912 | tf_op jit(solution)/shard_map/convert_element_type | solution.py:90
  44.1 26.6 %all-gather.2.cloned.1.call-done = bf16[1,4096,512]{2,1,0:T(8,128)(2,1)} async-done(((bf16[1,2048,512]{2,1,0:T(8,128)(2,1)}), bf16[1,4096,512]{2,1,0:T(8,128)(2,1)}) %all-gather.2.cloned.1.call-update) | async-done | bytes 4194320 | tf_op jit(solution)/shard_map/all_gather | solution.py:46
  70.7 4.6 %fusion.20 = f32[2,256,4096]{2,1,0:T(8,128)S(1)} fusion(bf16[1,4096,512]{2,1,0:T(8,128)(2,1)} %all-gather.2.cloned.1.call-done, bf16[1,2,256,512]{3,2,1,0:T(8,128)(2,1)S(1)} %copy-done.2, pred[2,256]{1,0:T(4,128)(4,1)S(1)} %iota_compare_fusion), kind=kOutput, calls=%fused_computation.31 | convolution fusion | flops 2147745792 | bytes 13107712 | tf_op jit(solution)/shard_map/mtk,rk->mtr/dot_general | solution.py:43
  75.3 2.8 broadcast_in_dim.50
  78.1 2.5 fusion.27
  80.7 1.3 collective-permute-start
  82.0 1.8 constant_dynamic-slice_fusion.2
  83.8 46.2 %collective-permute-done = bf16[256,4096]{1,0:T(8,128)(2,1)} collective-permute-done((bf16[256,4096]{1,0:T(8,128)(2,1)S(1)}, bf16[256,4096]{1,0:T(8,128)(2,1)}, u32[]{:S(2)}, u32[]{:S(2)}) %collective-permute-start) | collective-permute-done | bytes 2097184 | tf_op jit(solution)/shard_map/ppermute | solution.py:19
  130.1 5.3 %bitcast_dynamic-update-slice_fusion.2 = (bf16[2,256,4096]{2,1,0:T(8,128)(2,1)}, bf16[256,4096]{1,0:T(8,128)(2,1)S(1)}) fusion(bf16[2,256,4096]{2,1,0:T(8,128)(2,1)} %get-tuple-element.89, s32[]{:T(128)S(6)} %min.17, bf16[1,256,4096]{2,1,0:T(8,128)(2,1)S(1)} %constant_dynamic-slice_fusion.2, pred[]{:T(512)S(6)} %and.26, f32[2,256,4096]{2,1,0:T(8,128)} %copy-done, ...), kind=kLoop, calls=%fused_computation.42 | loop fusion | flops 4194304 | bytes 12582917 | tf_op jit(solution)/shard_map/jit(dynamic_update_index_in_dim)/dynamic_update_slice | solution.py:61
  135.4 1.3 collective-permute-start.1
  136.7 1.8 constant_dynamic-slice_fusion.1
  138.5 45.4 %collective-permute-done.1 = bf16[256,4096]{1,0:T(8,128)(2,1)} collective-permute-done((bf16[256,4096]{1,0:T(8,128)(2,1)S(1)}, bf16[256,4096]{1,0:T(8,128)(2,1)}, u32[]{:S(2)}, u32[]{:S(2)}) %collective-permute-start.1) | collective-permute-done | bytes 2097184 | tf_op jit(solution)/shard_map/ppermute | solution.py:19
  183.9 5.3 %bitcast_dynamic-update-slice_fusion.1 = (bf16[2,256,4096]{2,1,0:T(8,128)(2,1)}, bf16[256,4096]{1,0:T(8,128)(2,1)S(1)}) fusion(bf16[2,256,4096]{2,1,0:T(8,128)(2,1)} %get-tuple-element.86, s32[]{:T(128)S(6)} %min.18, bf16[1,256,4096]{2,1,0:T(8,128)(2,1)S(1)} %constant_dynamic-slice_fusion.1, pred[]{:T(512)S(6)} %and.27, f32[2,256,4096]{2,1,0:T(8,128)} %copy-done, ...), kind=kLoop, calls=%fused_computation.40 | loop fusion | flops 4194304 | bytes 12582917 | tf_op jit(solution)/shard_map/jit(dynamic_update_index_in_dim)/dynamic_update_slice | solution.py:61
  189.2 1.3 collective-permute-start.2
  190.6 1.8 constant_dynamic-slice_fusion
  192.4 44.4 %collective-permute-done.2 = bf16[256,4096]{1,0:T(8,128)(2,1)} collective-permute-done((bf16[256,4096]{1,0:T(8,128)(2,1)S(1)}, bf16[256,4096]{1,0:T(8,128)(2,1)}, u32[]{:S(2)}, u32[]{:S(2)}) %collective-permute-start.2) | collective-permute-done | bytes 2097184 | tf_op jit(solution)/shard_map/ppermute | solution.py:19
  236.8 5.4 %bitcast_dynamic-update-slice_fusion = (bf16[2,256,4096]{2,1,0:T(8,128)(2,1)}, bf16[256,4096]{1,0:T(8,128)(2,1)S(1)}) fusion(bf16[2,256,4096]{2,1,0:T(8,128)(2,1)} %get-tuple-element.84, s32[]{:T(128)S(6)} %min.19, bf16[1,256,4096]{2,1,0:T(8,128)(2,1)S(1)} %constant_dynamic-slice_fusion, pred[]{:T(512)S(6)} %and.28, f32[2,256,4096]{2,1,0:T(8,128)} %copy-done, ...), kind=kLoop, calls=%fused_computation.38 | loop fusion | flops 4194304 | bytes 12582917 | tf_op jit(solution)/shard_map/jit(dynamic_update_index_in_dim)/dynamic_update_slice | solution.py:61
  242.2 1.5 collective-permute-start.3
  243.7 0.8 all-reduce.2.cloned.1.call-done
  244.5 11.6 %fusion.26 = (f32[1,2048,512]{2,1,0:T(8,128)}, f32[1,2048,512]{2,1,0:T(8,128)}, f32[1,2048,512]{2,1,0:T(8,128)}) fusion(bf16[2048,512]{1,0:T(8,128)(2,1)} %all-reduce.2.cloned.1.call-done, f32[1,2048,512]{2,1,0:T(8,128)} %param.15, f32[1,2048,512]{2,1,0:T(8,128)} %param.14, f32[1,2048,512]{2,1,0:T(8,128)} %param.13), kind=kLoop, calls=%fused_computation.44 | loop fusion | flops 17825792 | bytes 27262976 | tf_op jit(solution)/shard_map/broadcast_in_dim | solution.py:96
  256.1 2.2 copy.14
  258.3 30.5 %collective-permute-done.3 = bf16[256,4096]{1,0:T(8,128)(2,1)} collective-permute-done((bf16[256,4096]{1,0:T(8,128)(2,1)S(1)}, bf16[256,4096]{1,0:T(8,128)(2,1)}, u32[]{:S(2)}, u32[]{:S(2)}) %collective-permute-start.3) | collective-permute-done | bytes 2097184 | tf_op jit(solution)/shard_map/ppermute | solution.py:19
  288.8 4.5 %fusion.25 = bf16[1,2,256,4096]{3,2,1,0:T(8,128)(2,1)S(1)} fusion(bf16[1,2,256,4096]{3,2,1,0:T(8,128)(2,1)S(1)} %copy.14, s32[]{:T(128)S(6)} %min.20, f32[2,256,4096]{2,1,0:T(8,128)} %copy-done, bf16[256,4096]{1,0:T(8,128)(2,1)} %collective-permute-done.3, bf16[2,256,4096]{2,1,0:T(8,128)(2,1)} %get-tuple-element.82, pred[]{:T(512)S(6)} %and.29), kind=kLoop, calls=%fused_computation.37 | loop fusion | flops 4194304 | bytes 10485765 | tf_op jit(solution)/shard_map/jit(dynamic_update_index_in_dim)/dynamic_update_slice | solution.py:61
  293.3 2.0 copy-done.1
  (19 shorter events, 1.1 us)
Async XLA Ops:
  7.2 4.0 %copy-start.3 = (s32[1,2]{1,0:T(1,128)S(1)}, s32[1,2]{1,0:T(1,128)}, u32[]{:S(2)}) copy-start(s32[1,2]{1,0:T(1,128)} %param.12) | copy-start | bytes 28
  7.2 5.9 %copy-start.2 = (bf16[1,2,256,512]{3,2,1,0:T(8,128)(2,1)S(1)}, bf16[1,2,256,512]{3,2,1,0:T(8,128)(2,1)}, u32[]{:S(2)}) copy-start(bf16[1,2,256,512]{3,2,1,0:T(8,128)(2,1)} %param.11) | copy-start | bytes 1572868
  7.2 63.5 %all-gather.2.cloned.1.call-start = ((), (), s32[]{:S(2)}) async-start(), calls=%async_computation.1 | async-start | bytes 6291456 | tf_op jit(solution)/shard_map/all_gather | solution.py:46
  11.1 179.5 %reduce-scatter.2.cloned.1.call-start = ((), (), s32[]{:S(2)}) async-start(), calls=%async_computation.2 | async-start | bytes 6291456 | tf_op jit(solution)/shard_map/reduce_scatter | solution.py:89
  44.0 200.5 %all-reduce.2.cloned.1.call-start = ((), (), s32[]{:S(2)}) async-start(), calls=%async_computation.3 | async-start | bytes 4194304 | tf_op jit(solution)/shard_map/psum | solution.py:92
  75.3 5.4 %copy-start = (f32[2,256,4096]{2,1,0:T(8,128)}, f32[2,256,4096]{2,1,0:T(8,128)S(1)}, u32[]{:S(2)}) copy-start(f32[2,256,4096]{2,1,0:T(8,128)S(1)} %fusion.20) | copy-start | bytes 25165828
  80.7 49.4 %collective-permute-start = (bf16[256,4096]{1,0:T(8,128)(2,1)S(1)}, bf16[256,4096]{1,0:T(8,128)(2,1)}, u32[]{:S(2)}, u32[]{:S(2)}) collective-permute-start(bf16[256,4096]{1,0:T(8,128)(2,1)S(1)} %get-tuple-element.88), channel_id=1, source_target_pairs={{8,0},{16,8},{24,16},{9,1},{17,9},{25,17},{10,2},{18,10},{26,18},{... | collective-permute-start | bytes 6291464 | tf_op jit(solution)/shard_map/ppermute | solution.py:19
  135.4 48.5 %collective-permute-start.1 = (bf16[256,4096]{1,0:T(8,128)(2,1)S(1)}, bf16[256,4096]{1,0:T(8,128)(2,1)}, u32[]{:S(2)}, u32[]{:S(2)}) collective-permute-start(bf16[256,4096]{1,0:T(8,128)(2,1)S(1)} %get-tuple-element.87), channel_id=1, source_target_pairs={{8,0},{16,8},{24,16},{9,1},{17,9},{25,17},{10,2},{18,10},{26,18},{... | collective-permute-start | bytes 6291464 | tf_op jit(solution)/shard_map/ppermute | solution.py:19
  189.2 47.6 %collective-permute-start.2 = (bf16[256,4096]{1,0:T(8,128)(2,1)S(1)}, bf16[256,4096]{1,0:T(8,128)(2,1)}, u32[]{:S(2)}, u32[]{:S(2)}) collective-permute-start(bf16[256,4096]{1,0:T(8,128)(2,1)S(1)} %get-tuple-element.85), channel_id=1, source_target_pairs={{8,0},{16,8},{24,16},{9,1},{17,9},{25,17},{10,2},{18,10},{26,18},{... | collective-permute-start | bytes 6291464 | tf_op jit(solution)/shard_map/ppermute | solution.py:19
  242.2 46.6 %collective-permute-start.3 = (bf16[256,4096]{1,0:T(8,128)(2,1)S(1)}, bf16[256,4096]{1,0:T(8,128)(2,1)}, u32[]{:S(2)}, u32[]{:S(2)}) collective-permute-start(bf16[256,4096]{1,0:T(8,128)(2,1)S(1)} %get-tuple-element.83), channel_id=1, source_target_pairs={{8,0},{16,8},{24,16},{9,1},{17,9},{25,17},{10,2},{18,10},{26,18},{... | collective-permute-start | bytes 6291464 | tf_op jit(solution)/shard_map/ppermute | solution.py:19
  293.3 2.0 copy-start.1
Sparse Core Ops, SparseCore 0:
  11.2 59.4 all-gather.1
  73.5 54.2 reduce-scatter.1
  190.7 53.7 all-reduce.1
where the time goes:
time: 303 us; the launch traced here: 302 us
  waiting for transfers between devices  194 us (64%)
  other arithmetic  44.7 us (15%)
  matrix products  21.5 us (7%)
  local copies, waits for them, and re-layouts  20.9 us (7%)
  between operations  15.3 us (5%)
  starting transfers between devices  5.42 us (2%)
    ppermute x4, waiting for transfers between devices, passed_along(): return lax.ppermute(array, axis, pairs)  167 us
    all_gather x1, waiting for transfers between devices, local(): lax.all_gather(weight_half, 'fsdp', axis=1, tiled=True)[0]  26.6 us
    dynamic_update_slice x4, other arithmetic, local(): lax.dynamic_update_index_in_dim(grad_buffer, jnp.where(active, result, cu...  20.6 us
    dot_general x2, matrix products, accumulate(): lax.dot_general(inputs_block, grads_block, (((0,), (0,)), ((), ())), pref...  16.9 us
    broadcast_in_dim x1, other arithmetic, local(): new_second[None]  11.6 us
  transfers between devices with their start and end apart: 7, of which 6 were waited for; matrix products, arithmetic and copies ran while one was open for 25% of the time, Pallas kernels for 0%

commit v1 on v0

v1 whole, which is shorter than its diff:
```python
import functools

import jax
import jax.numpy as jnp
from jax import lax
from jax.experimental import pallas as pl
from jax.experimental.pallas import tpu as pltpu
from jax.sharding import PartitionSpec as P

beta_one = 0.9
beta_two = 0.95
learn_rate = 0.01
decay_rate = 0.1
adam_eps = 1e-08
loss_scale = 256.0
first_bias = 1.0 - 0.9**10
second_bias = 1.0 - 0.95**10

MESH = pl.DeviceIdType.MESH
COLS = 128


def adamw_update(weight_part, first_part, second_part, gradient):
    first_next = beta_one * first_part + (1.0 - beta_one) * gradient
    second_next = beta_two * second_part + (1.0 - beta_two) * gradient * gradient
    first_hat = first_next / first_bias
    second_hat = second_next / second_bias
    weight_next = weight_part - learn_rate * (
        first_hat / (jnp.sqrt(second_hat) + adam_eps) + decay_rate * weight_part
    )
    return (weight_next, first_next, second_next)


def kernel(
    n_pipe, n_dp, n_fsdp,
    counts, x_hbm, k_hbm, w_hbm,
    out_hbm, grad_hbm,
    x, k, km, wstage, wfull, inc, res, mine, psend, precv, ysend, yrecv, xsend, xrecv, grad,
    load_sem, chain_send, chain_recv, out_sem,
    w_send, w_recv, wf_send, wf_recv,
    p_send, p_recv, y_send, y_recv, x_send, x_recv, g_send, g_recv, grad_sem,
):
    micro, tokens, _ = x.shape
    width = k.shape[-1]
    rows = w_hbm.shape[1]
    half = rows // 2
    per_shard = micro * (rows // COLS)
    n_chunks = n_fsdp * per_shard
    per_half = half // COLS
    n_pieces = n_fsdp * per_half

    s = lax.axis_index("pipe")
    d = lax.axis_index("dp")
    f = lax.axis_index("fsdp")
    core = lax.rem(d, 2)
    core_peer = d + 1 - 2 * core
    far_peer = lax.rem(d + 2, n_dp)

    def remote(src, dst, send, recv, **where):
        return pltpu.make_async_remote_copy(
            src_ref=src, dst_ref=dst, send_sem=send, recv_sem=recv,
            device_id=where, device_id_type=MESH,
        )

    load_k = pltpu.make_async_copy(k_hbm.at[0], k, load_sem.at[0])
    load_w = pltpu.make_async_copy(w_hbm.at[0], wstage, load_sem.at[1])
    load_x = pltpu.make_async_copy(x_hbm.at[0], x, load_sem.at[2])
    load_k.start()
    load_w.start()
    load_x.start()

    barrier = pltpu.get_barrier_semaphore()
    pl.semaphore_signal(barrier, inc=1, device_id={"dp": core_peer}, device_id_type=MESH)
    pl.semaphore_signal(barrier, inc=1, device_id={"dp": far_peer}, device_id_type=MESH)
    for i in range(1, n_fsdp):
        pl.semaphore_signal(
            barrier, inc=1, device_id={"fsdp": lax.rem(f + i, n_fsdp)}, device_id_type=MESH
        )

    @pl.when(s > 0)
    def _():
        pl.semaphore_signal(barrier, inc=1, device_id={"pipe": s - 1}, device_id_type=MESH)

    @pl.when(s < n_pipe - 1)
    def _():
        pl.semaphore_signal(barrier, inc=1, device_id={"pipe": s + 1}, device_id_type=MESH)

    load_k.wait()
    for m in range(micro):
        live = lax.broadcasted_iota(jnp.int32, (tokens, width), 0) < counts[0, m]
        km[m * tokens:(m + 1) * tokens, :] = jnp.where(live, k[m], jnp.zeros_like(k[m]))
    load_w.wait()

    def convert(i, _):
        at = pl.ds(pl.multiple_of(i * COLS, COLS), COLS)
        wfull[f, at, :] = wstage[at, :].astype(jnp.bfloat16)
        return 0

    lax.fori_loop(0, rows // COLS, convert, 0)

    neighbours = n_fsdp + 1 + jnp.minimum(s, 1) + jnp.minimum(n_pipe - 1 - s, 1)
    pl.semaphore_wait(barrier, neighbours)

    my_half = pl.ds(pl.multiple_of(core * half, half), half)

    def w_copy(i):
        return remote(
            wfull.at[f, my_half], wfull.at[f, my_half], w_send.at[i - 1], w_recv.at[i - 1],
            fsdp=lax.rem(f + i, n_fsdp),
        )

    def w_forward(i):
        source = lax.rem(f + n_fsdp - i, n_fsdp)
        return remote(
            wfull.at[source, my_half], wfull.at[source, my_half],
            wf_send.at[i - 1], wf_recv.at[i - 1], dp=core_peer,
        )

    for i in range(1, n_fsdp):
        w_copy(i).start()
    load_x.wait()

    def chain_copy(j):
        return remote(res.at[j], inc.at[j], chain_send.at[j], chain_recv.at[j], pipe=s - 1)

    def place(j):
        shard = lax.rem(f + j // per_shard, n_fsdp)
        within = lax.rem(j, per_shard)
        return shard, within // micro, lax.rem(within, micro)

    def out_copy(j):
        shard, block, m = place(j)
        at = pl.ds(pl.multiple_of(shard * rows + block * COLS, COLS), COLS)
        return pltpu.make_async_copy(res.at[j], out_hbm.at[0, m, :, at], out_sem.at[j])

    def chain_step(j):
        shard, block, m = place(j)
        w_block = wfull[shard, pl.ds(pl.multiple_of(block * COLS, COLS), COLS), :]
        k_block = km[pl.ds(pl.multiple_of(m * tokens, tokens), tokens), :]
        term = lax.dot_general(
            k_block, w_block, (((1,), (1,)), ((), ())), preferred_element_type=jnp.float32
        )

        @pl.when(s < n_pipe - 1)
        def _():
            chain_copy(j).wait_recv()
            res[j] = (inc[j].astype(jnp.float32) + term).astype(jnp.bfloat16)

        @pl.when(s == n_pipe - 1)
        def _():
            res[j] = term.astype(jnp.bfloat16)

        @pl.when(s > 0)
        def _():
            chain_copy(j).start()

        out_copy(j).start()

    def piece_at(q):
        return q // per_half, pl.ds(pl.multiple_of(lax.rem(q, per_half) * COLS, COLS), COLS)

    def product(q, which):
        shard = q // per_half
        start = shard * rows + which * half + lax.rem(q, per_half) * COLS
        x_block = x[:, :, pl.ds(pl.multiple_of(start, COLS), COLS)].reshape(micro * tokens, COLS)
        return lax.dot_general(
            x_block, km[...], (((0,), (0,)), ((), ())), preferred_element_type=jnp.float32
        )

    def piece_copy(q):
        shard, at = piece_at(q)
        return remote(
            psend.at[shard, at], precv.at[shard, at], p_send.at[q], p_recv.at[q], dp=core_peer
        )

    def peer_piece(q):
        shard, at = piece_at(q)
        psend[shard, at, :] = product(q, 1 - core).astype(jnp.bfloat16)
        piece_copy(q).start()

    def own_piece(q):
        shard, at = piece_at(q)
        mine[shard, at, :] = product(q, core)

    def y_copy(i):
        return remote(
            ysend.at[i - 1], yrecv.at[i - 1], y_send.at[i - 1], y_recv.at[i - 1],
            fsdp=lax.rem(f + i, n_fsdp),
        )

    x_copy = remote(xsend, xrecv, x_send, x_recv, dp=far_peer)
    g_copy = remote(grad.at[my_half], grad.at[my_half], g_send, g_recv, dp=core_peer)

    def blocks(body):
        def step(b, _):
            body(pl.ds(pl.multiple_of(b * COLS, COLS), COLS), b)
            return 0

        lax.fori_loop(0, per_half, step, 0)

    def sum_pair():
        def wait(q, _):
            piece_copy(q).wait_recv()
            return 0

        lax.fori_loop(0, n_pieces, wait, 0)
        for i in range(1, n_fsdp):
            shard = lax.rem(f + i, n_fsdp)

            def add(at, b, i=i, shard=shard):
                ysend[i - 1, at, :] = (
                    mine[shard, at, :] + precv[shard, at, :].astype(jnp.float32)
                ).astype(jnp.bfloat16)

            blocks(add)
            y_copy(i).start()

    def sum_fsdp():
        for i in range(1, n_fsdp):
            y_copy(i).wait_recv()

        def add(at, b):
            total = mine[f, at, :] + precv[f, at, :].astype(jnp.float32)
            for i in range(1, n_fsdp):
                total = total + yrecv[i - 1, at, :].astype(jnp.float32)
            xsend[at, :] = total.astype(jnp.bfloat16)

        blocks(add)
        x_copy.start()

    def sum_far():
        x_copy.wait_recv()

        def add(at, b):
            to = pl.ds(pl.multiple_of(core * half + b * COLS, COLS), COLS)
            grad[to, :] = (
                xsend[at, :].astype(jnp.float32) + xrecv[at, :].astype(jnp.float32)
            ) / loss_scale

        blocks(add)
        g_copy.start()

    def forward_weights():
        for i in range(1, n_fsdp):
            w_copy(i).wait_recv()
            w_forward(i).start()

    def weights_here():
        for i in range(1, n_fsdp):
            w_forward(i).wait_recv()

    steps_a = n_pieces // 2

    def run(first, last):
        def step(j, _):
            chain_step(j)
            if last <= steps_a:
                peer_piece(2 * j)
                peer_piece(2 * j + 1)
            elif last <= 2 * steps_a:
                own_piece(2 * (j - steps_a))
                own_piece(2 * (j - steps_a) + 1)
            return 0

        if last > first:
            lax.fori_loop(first, last, step, 0)

    events = [
        (min(20, per_shard - 1), forward_weights),
        (per_shard, weights_here),
        (steps_a, None),
        (2 * steps_a, None),
        (2 * steps_a + 2, sum_pair),
        (44, sum_fsdp),
        (60, sum_far),
    ]
    done = 0
    for when, event in sorted(events, key=lambda pair: pair[0]):
        run(done, when)
        done = when
        if event is not None:
            event()
    run(done, n_chunks)

    g_copy.wait_recv()
    store_grad = pltpu.make_async_copy(grad, grad_hbm.at[0], grad_sem)
    store_grad.start()

    def finish(j, _):
        @pl.when(s > 0)
        def _():
            chain_copy(j).wait_send()

        out_copy(j).wait()
        return 0

    lax.fori_loop(0, n_chunks, finish, 0)

    def finish_pieces(q, _):
        piece_copy(q).wait_send()
        return 0

    lax.fori_loop(0, n_pieces, finish_pieces, 0)
    for i in range(1, n_fsdp):
        w_copy(i).wait_send()
        w_forward(i).wait_send()
        y_copy(i).wait_send()
    x_copy.wait_send()
    g_copy.wait_send()
    store_grad.wait()


def local(mesh, layer_inputs, key_grads, token_counts, master_weight, first_moment, second_moment):
    n_pipe, n_dp, n_fsdp = (mesh.shape[name] for name in ("pipe", "dp", "fsdp"))
    _, micro, tokens, features = layer_inputs.shape
    width = key_grads.shape[-1]
    rows = master_weight.shape[1]
    half = rows // 2
    n_chunks = micro * features // COLS
    n_pieces = n_fsdp * half // COLS
    others = n_fsdp - 1
    half_bf = (half, width)
    bf, f32 = jnp.bfloat16, jnp.float32
    dma = pltpu.SemaphoreType.DMA
    anywhere = pl.BlockSpec(memory_space=pl.ANY)
    input_grads, gradient = pl.pallas_call(
        functools.partial(kernel, n_pipe, n_dp, n_fsdp),
        out_shape=(
            jax.ShapeDtypeStruct(layer_inputs.shape, bf),
            jax.ShapeDtypeStruct(master_weight.shape, f32),
        ),
        in_specs=[pl.BlockSpec(memory_space=pltpu.SMEM), anywhere, anywhere, anywhere],
        out_specs=(anywhere, anywhere),
        scratch_shapes=[
            pltpu.VMEM((micro, tokens, features), bf),
            pltpu.VMEM((micro, tokens, width), bf),
            pltpu.VMEM((micro * tokens, width), bf),
            pltpu.VMEM((rows, width), f32),
            pltpu.VMEM((n_fsdp, rows, width), bf),
            pltpu.VMEM((n_chunks, tokens, COLS), bf),
            pltpu.VMEM((n_chunks, tokens, COLS), bf),
            pltpu.VMEM((n_fsdp,) + half_bf, f32),
            pltpu.VMEM((n_fsdp,) + half_bf, bf),
            pltpu.VMEM((n_fsdp,) + half_bf, bf),
            pltpu.VMEM((others,) + half_bf, bf),
            pltpu.VMEM((others,) + half_bf, bf),
            pltpu.VMEM(half_bf, bf),
            pltpu.VMEM(half_bf, bf),
            pltpu.VMEM((rows, width), f32),
            dma((3,)),
            dma((n_chunks,)), dma((n_chunks,)), dma((n_chunks,)),
            dma((others,)), dma((others,)), dma((others,)), dma((others,)),
            dma((n_pieces,)), dma((n_pieces,)),
            dma((others,)), dma((others,)),
            dma, dma, dma, dma, dma,
        ],
        compiler_params=pltpu.CompilerParams(
            collective_id=0, has_side_effects=True, vmem_limit_bytes=48 * 1024 * 1024
        ),
        cost_estimate=pl.CostEstimate(
            flops=4 * micro * tokens * width * features,
            bytes_accessed=32 * 1024 * 1024,
            transcendentals=0,
        ),
    )(token_counts, layer_inputs, key_grads, master_weight)
    new_weight, new_first, new_second = adamw_update(
        master_weight, first_moment, second_moment, gradient
    )
    return (input_grads, new_weight, new_first, new_second)


def solution(mesh):
    in_specs = (
        P("pipe", None, ("dp", "fsdp"), None),
        P("pipe", None, ("dp", "fsdp"), None),
        P("pipe", ("dp", "fsdp")),
        P("pipe", "fsdp", None),
        P("pipe", "fsdp", None),
        P("pipe", "fsdp", None),
    )
    out_specs = (
        P("pipe", None, ("dp", "fsdp"), None),
        P("pipe", "fsdp", None),
        P("pipe", "fsdp", None),
        P("pipe", "fsdp", None),
    )
    return jax.shard_map(
        functools.partial(local, mesh), mesh=mesh, in_specs=in_specs, out_specs=out_specs,
        check_vma=False,
    )
```

time: 303 us -> 124 us (0.41)
  waiting for transfers between devices: 194 us -> 0 us
  Pallas kernels: 0 us -> 111 us
  other arithmetic: 44.7 us -> 8 us
  matrix products: 21.5 us -> 0 us
  local copies, waits for them, and re-layouts: 20.9 us -> 3.71 us
  between operations: 15.3 us -> 0.67 us
  starting transfers between devices: 5.42 us -> 0 us
    ppermute x4 -> x0, waiting for transfers between devices: 167 us -> none  [passed_along(): return lax.ppermute(array, axis, pairs)]
    pallas_call x0 -> x1, Pallas kernels: none -> 111 us  [local(): pl.pallas_call(functools.partial(kernel, n_pipe, n_dp, n_fsdp), out_shape...]
    all_gather x1 -> x0, waiting for transfers between devices: 26.6 us -> none  [local(): lax.all_gather(weight_half, 'fsdp', axis=1, tiled=True)[0]]
    dot_general x3 -> x0, matrix products: 21.5 us -> none  [the longest x2 16.9 us: accumulate(): lax.dot_general(inputs_block, grads_block, (((0,), (0,)), ((), ())), pref...]
    dynamic_update_slice x4 -> x0, other arithmetic: 20.6 us -> none  [local(): lax.dynamic_update_index_in_dim(grad_buffer, jnp.where(active, result, cu...]
    convert_element_type x3 -> x0, other arithmetic: 12.3 us -> none  [the longest x1 5.93 us: local(): running.astype(jnp.bfloat16)]
    broadcast_in_dim x1 -> x0, other arithmetic: 11.6 us -> none  [local(): new_second[None]]
    sub x0 -> x1, other arithmetic: none -> 8 us  [adamw_update(): weight_part - learn_rate * (first_hat / (jnp.sqrt(second_hat) + adam_eps)...]
  transfers between devices with their start and end apart: 7 -> 0, of which waited for: 6 -> 0; matrix products, arithmetic and copies ran while one was open for 25% -> 0% of each run, Pallas kernels for 0% -> 0%
where the time goes in v1:
time: 124 us
  Pallas kernels  111 us (90%)
  other arithmetic  8 us (6%)
  local copies, waits for them, and re-layouts  3.71 us (3%)
    pallas_call x1, Pallas kernels, local(): pl.pallas_call(functools.partial(kernel, n_pipe, n_dp, n_fsdp), out_shape...  111 us
    sub x1, other arithmetic, adamw_update(): weight_part - learn_rate * (first_hat / (jnp.sqrt(second_hat) + adam_eps)...  8 us
    unnamed x9, local copies, waits for them, and re-layouts  3.71 us

profile of v1, /device:TPU:0, one launch (start us, length us, event | category | flops | bytes accessed | tf_op | source)
XLA Modules:
  0.0 123.5 jit_solution(8204103235028576200)
XLA Ops:
  0.6 0.0 copy-start
  0.6 1.0 copy-done
  1.7 0.0 copy-start.1
  1.7 0.7 copy-done.1
  2.3 0.0 copy-start.2
  2.3 0.0 copy-start.3
  2.3 111.2 %shard_map.93 = (bf16[1,2,256,4096]{3,2,1,0:T(8,128)(2,1)S(1)}, f32[1,2048,512]{2,1,0:T(8,128)}) custom-call(s32[1,2]{1,0:T(1,128)S(1)} %copy-done.1, bf16[1,2,256,4096]{3,2,1,0:T(8,128)(2,1)} %x_hbm.1, bf16[1,2,256,512]{3,2,1,0:T(8,128)(2,1)S(1)} %copy-done, f32[1,2048,512]{2,1,0:T(8,128)} %w_hbm.1), custom_call_target="tpu_custom_call" | custom-call | flops 4294967296 | bytes 33554432 | tf_op jit(solution)/shard_map/pallas_call | solution.py:326
  113.5 0.0 copy-done.2
  113.5 0.0 copy-done.3
  113.5 8.0 %multiply_subtract_fusion = (f32[1,2048,512]{2,1,0:T(8,128)}, f32[1,2048,512]{2,1,0:T(8,128)}, f32[1,2048,512]{2,1,0:T(8,128)}) fusion(f32[1,2048,512]{2,1,0:T(8,128)S(1)} %copy-done.2, f32[1,2048,512]{2,1,0:T(8,128)} %get-tuple-element.7, f32[1,2048,512]{2,1,0:T(8,128)S(1)} %copy-done.3, f32[1,2048,512]{2,1,0:T(8,128)} %param.11), kind=kLoop, calls=%fused_computation.2 | loop fusion | flops 15728640 | bytes 29360128 | tf_op jit(solution)/shard_map/sub | solution.py:28
  121.5 2.0 %copy.11 = bf16[1,2,256,4096]{3,2,1,0:T(8,128)(2,1)} copy(bf16[1,2,256,4096]{3,2,1,0:T(8,128)(2,1)S(1)} %get-tuple-element.15) | data formatting | bytes 8388608
Async XLA Ops:
  0.6 1.0 copy-start
  1.7 0.7 copy-start.1
  2.3 111.2 %copy-start.2 = (f32[1,2048,512]{2,1,0:T(8,128)S(1)}, f32[1,2048,512]{2,1,0:T(8,128)}, u32[]{:S(2)}) copy-start(f32[1,2048,512]{2,1,0:T(8,128)} %w_hbm.1) | copy-start | bytes 12582916
  2.3 111.2 %copy-start.3 = (f32[1,2048,512]{2,1,0:T(8,128)S(1)}, f32[1,2048,512]{2,1,0:T(8,128)}, u32[]{:S(2)}) copy-start(f32[1,2048,512]{2,1,0:T(8,128)} %param.10) | copy-start | bytes 12582916

commit v2 on v1

--- a/solution.py
+++ b/solution.py
@@ -17,6 +17,7 @@
 second_bias = 1.0 - 0.95**10
 
 MESH = pl.DeviceIdType.MESH
+IN_FLIGHT = 4
 COLS = 128
 
 
@@ -33,9 +34,9 @@
 
 def kernel(
     n_pipe, n_dp, n_fsdp,
-    counts, x_hbm, k_hbm, w_hbm,
+    counts_hbm, x_hbm, k_hbm, w_hbm,
     out_hbm, grad_hbm,
-    x, k, km, wstage, wfull, inc, res, mine, psend, precv, ysend, yrecv, xsend, xrecv, grad,
+    counts, x, k, km, wstage, wfull, inc, res, mine, psend, precv, ysend, yrecv, xsend, xrecv,
     load_sem, chain_send, chain_recv, out_sem,
     w_send, w_recv, wf_send, wf_recv,
     p_send, p_recv, y_send, y_recv, x_send, x_recv, g_send, g_recv, grad_sem,
@@ -44,6 +45,7 @@
     width = k.shape[-1]
     rows = w_hbm.shape[1]
     half = rows // 2
+    grad = wstage
     per_shard = micro * (rows // COLS)
     n_chunks = n_fsdp * per_shard
     per_half = half // COLS
@@ -63,10 +65,15 @@
         )
 
     load_k = pltpu.make_async_copy(k_hbm.at[0], k, load_sem.at[0])
-    load_w = pltpu.make_async_copy(w_hbm.at[0], wstage, load_sem.at[1])
+    load_counts = pltpu.make_async_copy(counts_hbm, counts, load_sem.at[3])
+    lead, rest = pl.ds(0, COLS), pl.ds(COLS, rows - COLS)
+    load_lead = pltpu.make_async_copy(w_hbm.at[0, lead], wstage.at[lead], load_sem.at[1])
+    load_rest = pltpu.make_async_copy(w_hbm.at[0, rest], wstage.at[rest], load_sem.at[4])
     load_x = pltpu.make_async_copy(x_hbm.at[0], x, load_sem.at[2])
+    load_counts.start()
     load_k.start()
-    load_w.start()
+    load_lead.start()
+    load_rest.start()
     load_x.start()
 
     barrier = pltpu.get_barrier_semaphore()
@@ -85,18 +92,13 @@
     def _():
         pl.semaphore_signal(barrier, inc=1, device_id={"pipe": s + 1}, device_id_type=MESH)
 
+    load_counts.wait()
     load_k.wait()
     for m in range(micro):
         live = lax.broadcasted_iota(jnp.int32, (tokens, width), 0) < counts[0, m]
         km[m * tokens:(m + 1) * tokens, :] = jnp.where(live, k[m], jnp.zeros_like(k[m]))
-    load_w.wait()
-
-    def convert(i, _):
-        at = pl.ds(pl.multiple_of(i * COLS, COLS), COLS)
-        wfull[f, at, :] = wstage[at, :].astype(jnp.bfloat16)
-        return 0
-
-    lax.fori_loop(0, rows // COLS, convert, 0)
+    load_lead.wait()
+    wfull[f, lead, :] = wstage[lead, :].astype(jnp.bfloat16)
 
     neighbours = n_fsdp + 1 + jnp.minimum(s, 1) + jnp.minimum(n_pipe - 1 - s, 1)
     pl.semaphore_wait(barrier, neighbours)
@@ -115,10 +117,6 @@
             wfull.at[source, my_half], wfull.at[source, my_half],
             wf_send.at[i - 1], wf_recv.at[i - 1], dp=core_peer,
         )
-
-    for i in range(1, n_fsdp):
-        w_copy(i).start()
-    load_x.wait()
 
     def chain_copy(j):
         return remote(res.at[j], inc.at[j], chain_send.at[j], chain_recv.at[j], pipe=s - 1)
@@ -156,6 +154,13 @@
 
         out_copy(j).start()
 
+    def chain_done(j):
+        @pl.when(s > 0)
+        def _():
+            chain_copy(j).wait_send()
+
+        out_copy(j).wait()
+
     def piece_at(q):
         return q // per_half, pl.ds(pl.multiple_of(lax.rem(q, per_half) * COLS, COLS), COLS)
 
@@ -240,6 +245,24 @@
         blocks(add)
         g_copy.start()
 
+        def finish_pieces(q, _):
+            piece_copy(q).wait_send()
+            return 0
+
+        lax.fori_loop(0, n_pieces, finish_pieces, 0)
+        for i in range(1, n_fsdp):
+            w_copy(i).wait_send()
+            w_forward(i).wait_send()
+            y_copy(i).wait_send()
+        x_copy.wait_send()
+
+    store_grad = pltpu.make_async_copy(grad, grad_hbm.at[0], grad_sem)
+
+    def gradient_here():
+        g_copy.wait_recv()
+        g_copy.wait_send()
+        store_grad.start()
+
     def forward_weights():
         for i in range(1, n_fsdp):
             w_copy(i).wait_recv()
@@ -253,7 +276,14 @@
 
     def run(first, last):
         def step(j, _):
-            chain_step(j)
+            @pl.when(j >= IN_FLIGHT)
+            def _():
+                chain_done(j - IN_FLIGHT)
+
+            @pl.when(jnp.logical_or(s < n_pipe - 1, j >= micro))
+            def _():
+                chain_step(j)
+
             if last <= steps_a:
                 peer_piece(2 * j)
                 peer_piece(2 * j + 1)
@@ -270,10 +300,28 @@
         (per_shard, weights_here),
         (steps_a, None),
         (2 * steps_a, None),
-        (2 * steps_a + 2, sum_pair),
-        (44, sum_fsdp),
-        (60, sum_far),
+        (2 * steps_a + 1, sum_pair),
+        (9 * n_chunks // 16, sum_fsdp),
+        (27 * n_chunks // 32, sum_far),
+        (31 * n_chunks // 32, gradient_here),
     ]
+
+    @pl.when(s == n_pipe - 1)
+    def _():
+        for j in range(micro):
+            chain_step(j)
+
+    load_rest.wait()
+
+    def convert(i, _):
+        at = pl.ds(pl.multiple_of(i * COLS, COLS), COLS)
+        wfull[f, at, :] = wstage[at, :].astype(jnp.bfloat16)
+        return 0
+
+    lax.fori_loop(1, rows // COLS, convert, 0)
+    for i in range(1, n_fsdp):
+        w_copy(i).start()
+    load_x.wait()
     done = 0
     for when, event in sorted(events, key=lambda pair: pair[0]):
         run(done, when)
@@ -282,31 +330,8 @@
             event()
     run(done, n_chunks)
 
-    g_copy.wait_recv()
-    store_grad = pltpu.make_async_copy(grad, grad_hbm.at[0], grad_sem)
-    store_grad.start()
-
-    def finish(j, _):
-        @pl.when(s > 0)
-        def _():
-            chain_copy(j).wait_send()
-
-        out_copy(j).wait()
-        return 0
-
-    lax.fori_loop(0, n_chunks, finish, 0)
-
-    def finish_pieces(q, _):
-        piece_copy(q).wait_send()
-        return 0
-
-    lax.fori_loop(0, n_pieces, finish_pieces, 0)
-    for i in range(1, n_fsdp):
-        w_copy(i).wait_send()
-        w_forward(i).wait_send()
-        y_copy(i).wait_send()
-    x_copy.wait_send()
-    g_copy.wait_send()
+    for j in range(max(n_chunks - IN_FLIGHT, 0), n_chunks):
+        chain_done(j)
     store_grad.wait()
 
 
@@ -329,9 +354,10 @@
             jax.ShapeDtypeStruct(layer_inputs.shape, bf),
             jax.ShapeDtypeStruct(master_weight.shape, f32),
         ),
-        in_specs=[pl.BlockSpec(memory_space=pltpu.SMEM), anywhere, anywhere, anywhere],
+        in_specs=[pl.BlockSpec(memory_space=pltpu.HBM)] * 4,
         out_specs=(anywhere, anywhere),
         scratch_shapes=[
+            pltpu.SMEM(token_counts.shape, jnp.int32),
             pltpu.VMEM((micro, tokens, features), bf),
             pltpu.VMEM((micro, tokens, width), bf),
             pltpu.VMEM((micro * tokens, width), bf),
@@ -346,8 +372,7 @@
             pltpu.VMEM((others,) + half_bf, bf),
             pltpu.VMEM(half_bf, bf),
             pltpu.VMEM(half_bf, bf),
-            pltpu.VMEM((rows, width), f32),
-            dma((3,)),
+            dma((5,)),
             dma((n_chunks,)), dma((n_chunks,)), dma((n_chunks,)),
             dma((others,)), dma((others,)), dma((others,)), dma((others,)),
             dma((n_pieces,)), dma((n_pieces,)),
@@ -355,14 +380,19 @@
             dma, dma, dma, dma, dma,
         ],
         compiler_params=pltpu.CompilerParams(
-            collective_id=0, has_side_effects=True, vmem_limit_bytes=48 * 1024 * 1024
+            collective_id=0, has_side_effects=True, vmem_limit_bytes=36 * 1024 * 1024
         ),
         cost_estimate=pl.CostEstimate(
             flops=4 * micro * tokens * width * features,
             bytes_accessed=32 * 1024 * 1024,
             transcendentals=0,
         ),
-    )(token_counts, layer_inputs, key_grads, master_weight)
+    )(
+        *[
+            pltpu.with_memory_space_constraint(array, pltpu.HBM)
+            for array in (token_counts, layer_inputs, key_grads, master_weight)
+        ]
+    )
     new_weight, new_first, new_second = adamw_update(
         master_weight, first_moment, second_moment, gradient
     )

time: 124 us -> 115 us (0.927)
  Pallas kernels: 111 us -> 106 us
  other arithmetic: 8 us -> 5.78 us
  local copies, waits for them, and re-layouts: 3.71 us -> 2.03 us
    pallas_call x1, Pallas kernels: 111 us -> 106 us  [local(): pl.pallas_call(functools.partial(kernel, n_pipe, n_dp, n_fsdp), out_shape...]
    sub x1, other arithmetic: 8 us -> 5.78 us  [adamw_update(): weight_part - learn_rate * (first_hat / (jnp.sqrt(second_hat) + adam_eps)...]
    unnamed x9 -> x7, local copies, waits for them, and re-layouts: 3.71 us -> 2.03 us
where the time goes in v2:
time: 115 us; the launch traced here: 114 us
  Pallas kernels  106 us (92%)
  other arithmetic  5.78 us (5%)
  local copies, waits for them, and re-layouts  2.03 us (2%)
    pallas_call x1, Pallas kernels, local(): pl.pallas_call(functools.partial(kernel, n_pipe, n_dp, n_fsdp), out_shape...  106 us
    sub x1, other arithmetic, adamw_update(): weight_part - learn_rate * (first_hat / (jnp.sqrt(second_hat) + adam_eps)...  5.78 us

profile of v2, /device:TPU:0, one launch (start us, length us, event | category | flops | bytes accessed | tf_op | source)
XLA Modules:
  0.0 114.4 jit_solution(1797404573310386311)
XLA Ops:
  0.6 0.0 copy-start
  0.6 0.0 copy-start.2
  0.7 0.0 copy-start.1
  0.7 105.9 %shard_map.93 = (bf16[1,2,256,4096]{3,2,1,0:T(8,128)(2,1)S(1)}, f32[1,2048,512]{2,1,0:T(8,128)S(1)}) custom-call(s32[1,2]{1,0:T(1,128)} %counts_hbm.1, bf16[1,2,256,4096]{3,2,1,0:T(8,128)(2,1)} %x_hbm.1, bf16[1,2,256,512]{3,2,1,0:T(8,128)(2,1)} %k_hbm.1, f32[1,2048,512]{2,1,0:T(8,128)} %w_hbm.1), custom_call_target="tpu_custom_call" | custom-call | flops 4294967296 | bytes 33554432 | tf_op jit(solution)/shard_map/pallas_call | solution.py:351
  106.6 0.0 copy-done
  106.6 0.0 copy-done.2
  106.6 0.0 copy-done.1
  106.6 5.8 %multiply_subtract_fusion = (f32[1,2048,512]{2,1,0:T(8,128)}, f32[1,2048,512]{2,1,0:T(8,128)}, f32[1,2048,512]{2,1,0:T(8,128)}) fusion(f32[1,2048,512]{2,1,0:T(8,128)S(1)} %copy-done, f32[1,2048,512]{2,1,0:T(8,128)S(1)} %get-tuple-element.7, f32[1,2048,512]{2,1,0:T(8,128)S(1)} %copy-done.1, f32[1,2048,512]{2,1,0:T(8,128)S(1)} %copy-done.2), kind=kLoop, calls=%fused_computation.2 | loop fusion | flops 15728640 | bytes 29360128 | tf_op jit(solution)/shard_map/sub | solution.py:29
  112.4 2.0 %copy.11 = bf16[1,2,256,4096]{3,2,1,0:T(8,128)(2,1)} copy(bf16[1,2,256,4096]{3,2,1,0:T(8,128)(2,1)S(1)} %get-tuple-element.15) | data formatting | bytes 8388608
Async XLA Ops:
  0.6 106.0 %copy-start = (f32[1,2048,512]{2,1,0:T(8,128)S(1)}, f32[1,2048,512]{2,1,0:T(8,128)}, u32[]{:S(2)}) copy-start(f32[1,2048,512]{2,1,0:T(8,128)} %w_hbm.1) | copy-start | bytes 12582916
  0.6 106.0 %copy-start.2 = (f32[1,2048,512]{2,1,0:T(8,128)S(1)}, f32[1,2048,512]{2,1,0:T(8,128)}, u32[]{:S(2)}) copy-start(f32[1,2048,512]{2,1,0:T(8,128)} %param.11) | copy-start | bytes 12582916
  0.7 106.0 %copy-start.1 = (f32[1,2048,512]{2,1,0:T(8,128)S(1)}, f32[1,2048,512]{2,1,0:T(8,128)}, u32[]{:S(2)}) copy-start(f32[1,2048,512]{2,1,0:T(8,128)} %param.10) | copy-start | bytes 12582916

commit v3 on v2

--- a/solution.py
+++ b/solution.py
@@ -162,10 +162,14 @@
         out_copy(j).wait()
 
     def piece_at(q):
-        return q // per_half, pl.ds(pl.multiple_of(lax.rem(q, per_half) * COLS, COLS), COLS)
+        shard = lax.rem(f + 1 + q // per_half, n_fsdp)
+        return shard, pl.ds(pl.multiple_of(lax.rem(q, per_half) * COLS, COLS), COLS)
+
+    def block_at(b):
+        return pl.ds(pl.multiple_of(b * COLS, COLS), COLS)
 
     def product(q, which):
-        shard = q // per_half
+        shard, _ = piece_at(q)
         start = shard * rows + which * half + lax.rem(q, per_half) * COLS
         x_block = x[:, :, pl.ds(pl.multiple_of(start, COLS), COLS)].reshape(micro * tokens, COLS)
         return lax.dot_general(
@@ -183,85 +187,82 @@
         psend[shard, at, :] = product(q, 1 - core).astype(jnp.bfloat16)
         piece_copy(q).start()
 
-    def own_piece(q):
+    def peer_pieces(t):
+        peer_piece(2 * t)
+        peer_piece(2 * t + 1)
+
+    def pair_sum(q):
         shard, at = piece_at(q)
-        mine[shard, at, :] = product(q, core)
-
-    def y_copy(i):
+        term = product(q, core)
+        piece_copy(q).wait_recv()
+        return term + precv[shard, at, :].astype(jnp.float32)
+
+    def y_copy(q):
+        i, at = q // per_half, block_at(lax.rem(q, per_half))
         return remote(
-            ysend.at[i - 1], yrecv.at[i - 1], y_send.at[i - 1], y_recv.at[i - 1],
-            fsdp=lax.rem(f + i, n_fsdp),
-        )
-
-    x_copy = remote(xsend, xrecv, x_send, x_recv, dp=far_peer)
-    g_copy = remote(grad.at[my_half], grad.at[my_half], g_send, g_recv, dp=core_peer)
-
-    def blocks(body):
-        def step(b, _):
-            body(pl.ds(pl.multiple_of(b * COLS, COLS), COLS), b)
-            return 0
-
-        lax.fori_loop(0, per_half, step, 0)
-
-    def sum_pair():
-        def wait(q, _):
-            piece_copy(q).wait_recv()
-            return 0
-
-        lax.fori_loop(0, n_pieces, wait, 0)
-        for i in range(1, n_fsdp):
-            shard = lax.rem(f + i, n_fsdp)
-
-            def add(at, b, i=i, shard=shard):
-                ysend[i - 1, at, :] = (
-                    mine[shard, at, :] + precv[shard, at, :].astype(jnp.float32)
-                ).astype(jnp.bfloat16)
-
-            blocks(add)
-            y_copy(i).start()
-
-    def sum_fsdp():
-        for i in range(1, n_fsdp):
-            y_copy(i).wait_recv()
-
-        def add(at, b):
-            total = mine[f, at, :] + precv[f, at, :].astype(jnp.float32)
-            for i in range(1, n_fsdp):
-                total = total + yrecv[i - 1, at, :].astype(jnp.float32)
-            xsend[at, :] = total.astype(jnp.bfloat16)
-
-        blocks(add)
-        x_copy.start()
-
-    def sum_far():
-        x_copy.wait_recv()
-
-        def add(at, b):
-            to = pl.ds(pl.multiple_of(core * half + b * COLS, COLS), COLS)
-            grad[to, :] = (
-                xsend[at, :].astype(jnp.float32) + xrecv[at, :].astype(jnp.float32)
-            ) / loss_scale
-
-        blocks(add)
-        g_copy.start()
-
-        def finish_pieces(q, _):
+            ysend.at[i, at], yrecv.at[i, at], y_send.at[q], y_recv.at[q],
+            fsdp=lax.rem(f + 1 + i, n_fsdp),
+        )
+
+    def others_piece(q):
+        ysend[q // per_half, block_at(lax.rem(q, per_half)), :] = pair_sum(q).astype(jnp.bfloat16)
+        y_copy(q).start()
+
+    n_others = (n_fsdp - 1) * per_half
+
+    def own_piece(b):
+        mine[block_at(b), :] = pair_sum(n_others + b)
+
+    def x_copy(b):
+        at = block_at(b)
+        return remote(xsend.at[at], xrecv.at[at], x_send.at[b], x_recv.at[b], dp=far_peer)
+
+    def g_copy(b):
+        at = block_at(core * per_half + b)
+        return remote(grad.at[at], grad.at[at], g_send.at[b], g_recv.at[b], dp=core_peer)
+
+    def sum_fsdp(b):
+        at = block_at(b)
+        total = mine[at, :]
+        for i in range(n_fsdp - 1):
+            y_copy(i * per_half + b).wait_recv()
+            total = total + yrecv[i, at, :].astype(jnp.float32)
+        xsend[at, :] = total.astype(jnp.bfloat16)
+        x_copy(b).start()
+
+    def sum_far(b):
+        at = block_at(b)
+        x_copy(b).wait_recv()
+        grad[block_at(core * per_half + b), :] = (
+            xsend[at, :].astype(jnp.float32) + xrecv[at, :].astype(jnp.float32)
+        ) / loss_scale
+        g_copy(b).start()
+
+    store_grad = pltpu.make_async_copy(grad, grad_hbm.at[0], grad_sem)
+
+    def gradient_here():
+        for b in range(per_half):
+            g_copy(b).wait_recv()
+            g_copy(b).wait_send()
+        store_grad.start()
+
+    def finish_pieces():
+        def piece(q, _):
             piece_copy(q).wait_send()
             return 0
 
-        lax.fori_loop(0, n_pieces, finish_pieces, 0)
+        lax.fori_loop(0, n_pieces, piece, 0)
+
+    def finish_others():
         for i in range(1, n_fsdp):
             w_copy(i).wait_send()
             w_forward(i).wait_send()
-            y_copy(i).wait_send()
-        x_copy.wait_send()
-
-    store_grad = pltpu.make_async_copy(grad, grad_hbm.at[0], grad_sem)
-
-    def gradient_here():
-        g_copy.wait_recv()
-        g_copy.wait_send()
-        store_grad.start()
+
+        def piece(q, _):
+            y_copy(q).wait_send()
+            return 0
+
+        lax.fori_loop(0, n_others, piece, 0)
 
     def forward_weights():
         for i in range(1, n_fsdp):
@@ -272,7 +273,13 @@
         for i in range(1, n_fsdp):
             w_forward(i).wait_recv()
 
-    steps_a = n_pieces // 2
+    works = [
+        (0, n_pieces // 2, peer_pieces),
+        (n_pieces // 2, n_others, others_piece),
+        (n_pieces // 2 + n_others, per_half, own_piece),
+        (9 * n_chunks // 16, per_half, sum_fsdp),
+        (27 * n_chunks // 32, per_half, sum_far),
+    ]
 
     def run(first, last):
         def step(j, _):
@@ -284,27 +291,23 @@
             def _():
                 chain_step(j)
 
-            if last <= steps_a:
-                peer_piece(2 * j)
-                peer_piece(2 * j + 1)
-            elif last <= 2 * steps_a:
-                own_piece(2 * (j - steps_a))
-                own_piece(2 * (j - steps_a) + 1)
+            for start, count, work in works:
+                if start <= first and last <= start + count:
+                    work(j - start)
             return 0
 
         if last > first:
             lax.fori_loop(first, last, step, 0)
 
     events = [
-        (min(20, per_shard - 1), forward_weights),
+        (min(7 * n_chunks // 16, per_shard - 1), forward_weights),
         (per_shard, weights_here),
-        (steps_a, None),
-        (2 * steps_a, None),
-        (2 * steps_a + 1, sum_pair),
-        (9 * n_chunks // 16, sum_fsdp),
-        (27 * n_chunks // 32, sum_far),
-        (31 * n_chunks // 32, gradient_here),
+        (n_chunks // 2 + 1, finish_pieces),
+        (13 * n_chunks // 16, finish_others),
+        (63 * n_chunks // 64, gradient_here),
     ]
+    for start, count, _ in works:
+        events += [(start, None), (start + count, None)]
 
     @pl.when(s == n_pipe - 1)
     def _():
@@ -330,6 +333,8 @@
             event()
     run(done, n_chunks)
 
+    for b in range(per_half):
+        x_copy(b).wait_send()
     for j in range(max(n_chunks - IN_FLIGHT, 0), n_chunks):
         chain_done(j)
     store_grad.wait()
@@ -343,6 +348,7 @@
     half = rows // 2
     n_chunks = micro * features // COLS
     n_pieces = n_fsdp * half // COLS
+    per_half = half // COLS
     others = n_fsdp - 1
     half_bf = (half, width)
     bf, f32 = jnp.bfloat16, jnp.float32
@@ -365,7 +371,7 @@
             pltpu.VMEM((n_fsdp, rows, width), bf),
             pltpu.VMEM((n_chunks, tokens, COLS), bf),
             pltpu.VMEM((n_chunks, tokens, COLS), bf),
-            pltpu.VMEM((n_fsdp,) + half_bf, f32),
+            pltpu.VMEM(half_bf, f32),
             pltpu.VMEM((n_fsdp,) + half_bf, bf),
             pltpu.VMEM((n_fsdp,) + half_bf, bf),
             pltpu.VMEM((others,) + half_bf, bf),
@@ -376,8 +382,8 @@
             dma((n_chunks,)), dma((n_chunks,)), dma((n_chunks,)),
             dma((others,)), dma((others,)), dma((others,)), dma((others,)),
             dma((n_pieces,)), dma((n_pieces,)),
-            dma((others,)), dma((others,)),
-            dma, dma, dma, dma, dma,
+            dma((others * per_half,)), dma((others * per_half,)),
+            dma((per_half,)), dma((per_half,)), dma((per_half,)), dma((per_half,)), dma,
         ],
         compiler_params=pltpu.CompilerParams(
             collective_id=0, has_side_effects=True, vmem_limit_bytes=36 * 1024 * 1024

time: 115 us -> 116 us (level)
    pallas_call x1, Pallas kernels: 106 us -> 107 us  [local(): pl.pallas_call(functools.partial(kernel, n_pipe, n_dp, n_fsdp), out_shape...]
where the time goes in v3:
time: 116 us
  Pallas kernels  107 us (92%)
  other arithmetic  5.78 us (5%)
  local copies, waits for them, and re-layouts  2.03 us (2%)
    pallas_call x1, Pallas kernels, local(): pl.pallas_call(functools.partial(kernel, n_pipe, n_dp, n_fsdp), out_shape...  107 us
    sub x1, other arithmetic, adamw_update(): weight_part - learn_rate * (first_hat / (jnp.sqrt(second_hat) + adam_eps)...  5.78 us

profile of v3, /device:TPU:0, one launch (start us, length us, event | category | flops | bytes accessed | tf_op | source)
XLA Modules:
  0.0 115.7 jit_solution(4967998416131363736)
XLA Ops:
  0.6 0.0 copy-start
  0.6 0.0 copy-start.2
  0.7 0.0 copy-start.1
  0.7 107.2 %shard_map.93 = (bf16[1,2,256,4096]{3,2,1,0:T(8,128)(2,1)S(1)}, f32[1,2048,512]{2,1,0:T(8,128)S(1)}) custom-call(s32[1,2]{1,0:T(1,128)} %counts_hbm.1, bf16[1,2,256,4096]{3,2,1,0:T(8,128)(2,1)} %x_hbm.1, bf16[1,2,256,512]{3,2,1,0:T(8,128)(2,1)} %k_hbm.1, f32[1,2048,512]{2,1,0:T(8,128)} %w_hbm.1), custom_call_target="tpu_custom_call" | custom-call | flops 4294967296 | bytes 33554432 | tf_op jit(solution)/shard_map/pallas_call | solution.py:357
  107.9 0.0 copy-done
  107.9 0.0 copy-done.2
  107.9 0.0 copy-done.1
  107.9 5.8 %multiply_subtract_fusion = (f32[1,2048,512]{2,1,0:T(8,128)}, f32[1,2048,512]{2,1,0:T(8,128)}, f32[1,2048,512]{2,1,0:T(8,128)}) fusion(f32[1,2048,512]{2,1,0:T(8,128)S(1)} %copy-done, f32[1,2048,512]{2,1,0:T(8,128)S(1)} %get-tuple-element.7, f32[1,2048,512]{2,1,0:T(8,128)S(1)} %copy-done.1, f32[1,2048,512]{2,1,0:T(8,128)S(1)} %copy-done.2), kind=kLoop, calls=%fused_computation.2 | loop fusion | flops 15728640 | bytes 29360128 | tf_op jit(solution)/shard_map/sub | solution.py:29
  113.7 2.0 %copy.11 = bf16[1,2,256,4096]{3,2,1,0:T(8,128)(2,1)} copy(bf16[1,2,256,4096]{3,2,1,0:T(8,128)(2,1)S(1)} %get-tuple-element.15) | data formatting | bytes 8388608
Async XLA Ops:
  0.6 107.2 %copy-start = (f32[1,2048,512]{2,1,0:T(8,128)S(1)}, f32[1,2048,512]{2,1,0:T(8,128)}, u32[]{:S(2)}) copy-start(f32[1,2048,512]{2,1,0:T(8,128)} %w_hbm.1) | copy-start | bytes 12582916
  0.6 107.2 %copy-start.2 = (f32[1,2048,512]{2,1,0:T(8,128)S(1)}, f32[1,2048,512]{2,1,0:T(8,128)}, u32[]{:S(2)}) copy-start(f32[1,2048,512]{2,1,0:T(8,128)} %param.11) | copy-start | bytes 12582916
  0.7 107.2 %copy-start.1 = (f32[1,2048,512]{2,1,0:T(8,128)S(1)}, f32[1,2048,512]{2,1,0:T(8,128)}, u32[]{:S(2)}) copy-start(f32[1,2048,512]{2,1,0:T(8,128)} %param.10) | copy-start | bytes 12582916

commit v4 on v2

--- a/solution.py
+++ b/solution.py
@@ -17,6 +17,7 @@
 second_bias = 1.0 - 0.95**10
 
 MESH = pl.DeviceIdType.MESH
+BLOCK = 512
 IN_FLIGHT = 4
 COLS = 128
 
@@ -30,6 +31,23 @@
         first_hat / (jnp.sqrt(second_hat) + adam_eps) + decay_rate * weight_part
     )
     return (weight_next, first_next, second_next)
+
+
+def update_kernel(
+    grads_in, weight, first, second, gradient, grads_out, new_weight, new_first, new_second, sem
+):
+    copy = pltpu.make_async_copy(grads_in, grads_out, sem)
+
+    @pl.when(pl.program_id(0) == 0)
+    def _():
+        copy.start()
+
+    updated = adamw_update(weight[...], first[...], second[...], gradient[...])
+    new_weight[...], new_first[...], new_second[...] = updated
+
+    @pl.when(pl.program_id(0) == pl.num_programs(0) - 1)
+    def _():
+        copy.wait()
 
 
 def kernel(
@@ -393,10 +411,21 @@
             for array in (token_counts, layer_inputs, key_grads, master_weight)
         ]
     )
-    new_weight, new_first, new_second = adamw_update(
-        master_weight, first_moment, second_moment, gradient
-    )
-    return (input_grads, new_weight, new_first, new_second)
+    block_rows = min(BLOCK, rows)
+    block = pl.BlockSpec((1, block_rows, width), lambda i: (0, i, 0))
+    state = jax.ShapeDtypeStruct(master_weight.shape, f32)
+    return pl.pallas_call(
+        update_kernel,
+        grid=(rows // block_rows,),
+        out_shape=(jax.ShapeDtypeStruct(layer_inputs.shape, bf), state, state, state),
+        in_specs=[anywhere, block, block, block, block],
+        out_specs=(anywhere, block, block, block),
+        scratch_shapes=[dma],
+        compiler_params=pltpu.CompilerParams(vmem_limit_bytes=24 * 1024 * 1024),
+        cost_estimate=pl.CostEstimate(
+            flops=20 * rows * width, bytes_accessed=36 * 1024 * 1024, transcendentals=rows * width
+        ),
+    )(input_grads, master_weight, first_moment, second_moment, gradient)
 
 
 def solution(mesh):

time: 115 us -> 114 us (level)
  Pallas kernels: 106 us -> 113 us
  other arithmetic: 5.78 us -> 0 us
  local copies, waits for them, and re-layouts: 2.03 us -> 0.01 us
    pallas_call x0 -> x1, Pallas kernels: none -> 6.88 us  [local(): pl.pallas_call(update_kernel, grid=(rows // block_rows,), out_shape=(jax....]
    sub x1 -> x0, other arithmetic: 5.78 us -> none  [adamw_update(): weight_part - learn_rate * (first_hat / (jnp.sqrt(second_hat) + adam_eps)...]
    unnamed x7 -> x6, local copies, waits for them, and re-layouts: 2.03 us -> 0.01 us
where the time goes in v4:
time: 114 us
  Pallas kernels  113 us (99%)
    pallas_call x1, Pallas kernels, local(): pl.pallas_call(functools.partial(kernel, n_pipe, n_dp, n_fsdp), out_shape...  106 us
    pallas_call x1, Pallas kernels, local(): pl.pallas_call(update_kernel, grid=(rows // block_rows,), out_shape=(jax....  6.88 us

profile of v4, /device:TPU:0, one launch (start us, length us, event | category | flops | bytes accessed | tf_op | source)
XLA Modules:
  0.0 113.5 jit_solution(17826350405138652111)
XLA Ops:
  0.6 0.0 copy-start
  0.6 0.0 copy-start.2
  0.7 0.0 copy-start.1
  0.7 105.9 %shard_map.93 = (bf16[1,2,256,4096]{3,2,1,0:T(8,128)(2,1)S(1)}, f32[1,2048,512]{2,1,0:T(8,128)S(1)}) custom-call(s32[1,2]{1,0:T(1,128)} %counts_hbm.1, bf16[1,2,256,4096]{3,2,1,0:T(8,128)(2,1)} %x_hbm.1, bf16[1,2,256,512]{3,2,1,0:T(8,128)(2,1)} %k_hbm.1, f32[1,2048,512]{2,1,0:T(8,128)} %weight.1), custom_call_target="tpu_custom_call" | custom-call | flops 4294967296 | bytes 33554432 | tf_op jit(solution)/shard_map/pallas_call | solution.py:369
  106.6 0.0 copy-done
  106.6 0.0 copy-done.2
  106.6 0.0 copy-done.1
  106.6 6.9 %shard_map.94 = (bf16[1,2,256,4096]{3,2,1,0:T(8,128)(2,1)}, f32[1,2048,512]{2,1,0:T(8,128)}, f32[1,2048,512]{2,1,0:T(8,128)}, f32[1,2048,512]{2,1,0:T(8,128)}) custom-call(bf16[1,2,256,4096]{3,2,1,0:T(8,128)(2,1)S(1)} %get-tuple-element.6.grads_in, f32[1,2048,512]{2,1,0:T(8,128)S(1)} %copy-done, f32[1,2048,512]{2,1,0:T(8,128)S(1)} %copy-done.1, ...), custom_call_target="tpu_custom_call" | custom-call | flops 20971520 | bytes 37748736 | tf_op jit(solution)/shard_map/pallas_call | solution.py:417
Async XLA Ops:
  0.6 106.0 %copy-start = (f32[1,2048,512]{2,1,0:T(8,128)S(1)}, f32[1,2048,512]{2,1,0:T(8,128)}, u32[]{:S(2)}) copy-start(f32[1,2048,512]{2,1,0:T(8,128)} %weight.1) | copy-start | bytes 12582916
  0.6 106.0 %copy-start.2 = (f32[1,2048,512]{2,1,0:T(8,128)S(1)}, f32[1,2048,512]{2,1,0:T(8,128)}, u32[]{:S(2)}) copy-start(f32[1,2048,512]{2,1,0:T(8,128)} %second.1) | copy-start | bytes 12582916
  0.7 106.0 %copy-start.1 = (f32[1,2048,512]{2,1,0:T(8,128)S(1)}, f32[1,2048,512]{2,1,0:T(8,128)}, u32[]{:S(2)}) copy-start(f32[1,2048,512]{2,1,0:T(8,128)} %first.1) | copy-start | bytes 12582916
